TPU v7x, 256 devices: a whole 4x4x8 slice. The times are simulated.
256 devices in a mesh: wide: 64 (over z, x, core), narrow: 4 (over y).
Axes of the slice: x: 4, y: 4, z: 8, core: 2. Of those that a mesh axis runs over, the one named last changes fastest.
Arguments:
- raw_record: bfloat16 [4, 32768, 8192], P('narrow', 'wide'), may hold values from -600 to 600
- filter_taps: bfloat16 [32], replicated, may hold values from -1 to 1
- health_mask: int32 [8192], replicated, may hold values from 0 to 1, as said below
- counts: int32 [64], replicated, may hold values from 8 to 64, as said below
- source_index: int32 [64], replicated, may hold values from 0 to 8191, as said below
Outputs:
- correlations: float32 [64, 8192, 256], P('narrow', 'wide')
Inputs may be any that keep to these rules, and one draw needn't show every extreme that they name: `health_mask`: the first channel of each block and every source channel are flagged 1. Block b's channels on the fibre are the counts[b] leading ones, b * 128 to b * 128 + counts[b] - 1; some block has exactly 64. `source_index`: every source channel lies on the fibre and is healthy; two sources may coincide.
All inputs are finite; a program needn't handle non-finite values.
Results may differ from a plain program's by a relative error of at most 0.013.
Values may be sent and summed in bfloat16 or wider, within the bound.
A program may use at most 128 MiB of HBM per device.

v0:
```python
import math

import jax
import jax.numpy as jnp
from jax import lax
from jax.sharding import PartitionSpec as P

C = 8192
BLOCK_CH = 128
Q = 2
L = 256
F = 128
K = 32
SRC = 64


def passed_along(block, axis, distance):
    devices = range(lax.axis_size(axis))
    route = [(i - distance, i) for i in devices if i - distance in devices]
    return lax.ppermute(block, axis, route)


def taps_matrix(filter_taps, row_count, factor_q):
    tap_count = filter_taps.shape[0]
    columns = tap_count - factor_q + factor_q * row_count
    row_ids = jnp.arange(row_count, dtype=jnp.int32)[:, None]
    col_ids = jnp.arange(columns, dtype=jnp.int32)[None, :]
    offset = tap_count - 1 + factor_q * row_ids - col_ids
    selector = (offset[:, :, None] == jnp.arange(tap_count, dtype=jnp.int32)[None, None, :]).astype(
        jnp.float32
    )
    return jnp.sum(selector * filter_taps.astype(jnp.float32)[None, None, :], axis=2).astype(
        jnp.bfloat16
    )


def dft_table(length, bin_count):
    freq_ids = jnp.arange(1, bin_count + 1, dtype=jnp.int32)[:, None]
    sample_ids = jnp.arange(length, dtype=jnp.int32)[None, :]
    phases = freq_ids * sample_ids % length
    angles = phases.astype(jnp.float32) * (2.0 * math.pi / length)
    return jnp.concatenate([jnp.cos(angles), -jnp.sin(angles)], axis=0).astype(jnp.bfloat16)


def lag_table(length, bin_count):
    freq_ids = jnp.arange(1, bin_count + 1, dtype=jnp.int32)[:, None]
    lag_ids = jnp.arange(length, dtype=jnp.int32)[None, :] - length // 2
    phases = freq_ids * lag_ids % length
    angles = phases.astype(jnp.float32) * (2.0 * math.pi / length)
    return jnp.stack([jnp.cos(angles), -jnp.sin(angles)], axis=0).astype(jnp.bfloat16)


def live_flags(health_mask, counts, block_width):
    slot_ids = jnp.arange(block_width, dtype=jnp.int32)[None, :]
    inside = (counts[:, None] > slot_ids).astype(jnp.int32).reshape(-1)
    return health_mask * inside


def spectrum(extended, matrix_taps, table_dft, weights):
    decimated = jnp.dot(matrix_taps, extended, preferred_element_type=jnp.float32)
    scaling = lax.rsqrt(jnp.mean(decimated * decimated, axis=0) + 1e-06)
    normed = (decimated * scaling[None, :]).astype(jnp.bfloat16)
    spectra = jnp.dot(table_dft, normed, preferred_element_type=jnp.float32)
    bin_count = spectra.shape[0] // 2
    powers = spectra[:bin_count] * spectra[:bin_count] + spectra[bin_count:] * spectra[bin_count:]
    levels = jnp.dot(powers, weights, precision=lax.Precision.HIGHEST) / jnp.sum(weights) + 1e-06
    inverse = lax.rsqrt(levels)
    return (spectra * jnp.concatenate([inverse, inverse])[:, None]).astype(jnp.bfloat16)


def cross_terms(sources, channels):
    turned = jnp.stack([-sources[:, 1], sources[:, 0]], axis=1)
    real_part = jnp.einsum("spfk,spfc->kfc", sources, channels, preferred_element_type=jnp.float32)
    imag_part = jnp.einsum("spfk,spfc->kfc", turned, channels, preferred_element_type=jnp.float32)
    return jnp.stack([real_part, imag_part], axis=1)


def body(raw_record, filter_taps, health_mask, counts, source_index):
    samples = raw_record[0]
    margin = K - Q
    previous = passed_along(samples[Q * L - margin :], "wide", 1)
    extended = jnp.concatenate([previous, samples], axis=0)
    living = live_flags(health_mask, counts, BLOCK_CH)
    weights = living.astype(jnp.float32)
    spectra = spectrum(extended, taps_matrix(filter_taps, L, Q), dft_table(L, F), weights)
    picked = jnp.take(spectra, source_index, axis=1)
    wide_count = lax.axis_size("wide")
    narrow_count = lax.axis_size("narrow")
    own_width = C // wide_count
    share_rows = SRC // narrow_count
    received = lax.all_to_all(spectra[None], "wide", split_axis=2, concat_axis=0, tiled=True)
    channels = received.reshape(wide_count, 2, F, own_width)
    portion = lax.all_gather(picked[None], "wide", axis=0, tiled=True)
    number = portion.shape[0]
    running = cross_terms(portion.reshape(number, 2, F, SRC), channels)
    share = lax.psum_scatter(
        running.astype(jnp.bfloat16), "narrow", scatter_dimension=0, tiled=True
    ).astype(jnp.float32)
    chan_ids = lax.axis_index("wide") * own_width + jnp.arange(own_width, dtype=jnp.int32)
    alive_cols = lax.dynamic_slice_in_dim(weights, lax.axis_index("wide") * own_width, own_width, 0)
    own_sources = lax.dynamic_slice_in_dim(
        source_index, lax.axis_index("narrow") * share_rows, share_rows, 0
    )
    distinct = (chan_ids[None, :] != own_sources[:, None]).astype(jnp.float32)
    masked = (share * alive_cols[None, None, None, :] * distinct[:, None, None, :]).astype(
        jnp.bfloat16
    )
    factor = 1.0 / math.sqrt(wide_count * narrow_count * F)
    return (
        jnp.einsum("kpfc,pft->kct", masked, lag_table(L, F), preferred_element_type=jnp.float32)
        * factor
    )


def solution(mesh):
    placed = (P("narrow", "wide", None), P(), P(), P(), P())
    return jax.shard_map(
        body, mesh=mesh, in_specs=placed, out_specs=P("narrow", "wide", None), check_vma=False
    )
```

profile of v0, /device:TPU:1, one launch (start us, length us, event | category | flops | bytes accessed | tf_op | source)
XLA Modules:
  0.0 339.9 jit_solution(5522910934209345735)
XLA Ops:
  6.5 1.2 slice_bitcast_fusion
  7.7 4.5 %collective-permute-start = (bf16[30,8192]{1,0:T(8,128)(2,1)S(1)}, bf16[30,8192]{1,0:T(8,128)(2,1)S(1)}, u32[]{:S(2)}, u32[]{:S(2)}) collective-permute-start(bf16[30,8192]{1,0:T(8,128)(2,1)S(1)} %slice_bitcast_fusion), channel_id=1, source_target_pairs={{0,4},{4,8},{8,12},{12,16},{16,20},{20,24},{24,28},{28,32},{32,36}... | collective-permute-start | bytes 1474568 | tf_op jit(solution)/shard_map/ppermute | solution.py:20
  12.2 0.7 convert_element_type.56
  12.9 0.6 cosine_convert_fusion.1
  13.6 1.4 fusion.57
  15.0 6.4 %select_reduce_fusion = bf16[256,542]{0,1:T(8,128)(2,1)S(1)} fusion(f32[32]{0:T(128)S(1)} %convert_element_type.56, s32[256,542]{0,1:T(8,128)S(1)} %iota_subtract_fusion), kind=kLoop, calls=%fused_computation.1 | loop fusion | flops 13181440 | bytes 832640 | tf_op jit(solution)/shard_map/reduce_sum | solution.py:32
  21.4 0.0 collective-permute-done
  21.5 6.3 %multiply_reduce_fusion = (f32[8192]{0:T(1024)S(1)}, f32[256,8192]{1,0:T(8,128)S(1)}) fusion(bf16[256,542]{0,1:T(8,128)(2,1)S(1)} %select_reduce_fusion, bf16[512,8192]{1,0:T(8,128)(2,1)} %bitcast.63, bf16[30,8192]{1,0:T(8,128)(2,1)S(1)} %collective-permute-done), kind=kOutput, calls=%fused_computation.9 | convolution fusion | flops 2295259136 | bytes 17579008 | tf_op jit(solution)/shard_map/dot_general | solution.py:60
  27.8 1.3 fusion.4
  29.1 0.0 copy-start
  29.1 4.2 %fusion.33 = f32[128]{0:T(128)S(1)} fusion(f32[8192,1]{0,1:T(1,128)S(1)} %bitcast.64, f32[256,8192]{1,0:T(8,128)S(1)} %fusion.4, f32[]{:T(128)} %get-tuple-element.5), kind=kOutput, calls=%fused_computation.34 | convolution fusion | flops 15728896 | bytes 8421892 | tf_op jit(solution)/shard_map/dot_general | solution.py:66
  33.3 0.0 copy-done
  33.4 2.9 fusion.61
  36.2 17.9 %copy.33 = bf16[1,256,8192]{1,0,2:T(2,128)(2,1)} copy(bf16[1,256,8192]{2,1,0:T(8,128)(2,1)} %fusion.61) | data formatting | bytes 8388608 | tf_op jit(solution)/shard_map/broadcast_in_dim | solution.py:91
  54.1 0.5 broadcast.295
  54.6 43.5 %reduce = bf16[8192,256]{1,0:T(8,128)(2,1)} reduce(bf16[8192,1,256]{2,1,0:T(2,128)(2,1)} %bitcast.58, bf16[]{:T(256)} %broadcast.295), dimensions={1}, to_apply=%bitcast.51.reduce_sub_computation | reduce | bytes 8388610
  98.1 6.9 %reshape.266 = bf16[64,2,16384]{2,1,0:T(2,128)(2,1)} reshape(bf16[8192,256]{1,0:T(8,128)(2,1)} %reduce) | data formatting | bytes 8388608
  105.0 0.0 copy-start.3
  105.0 11.6 %all-to-all-start = ((bf16[64,2,16384]{2,1,0:T(2,128)(2,1)}), bf16[64,2,16384]{2,1,0:T(2,128)(2,1)}, u32[]{:S(2)}, u32[]{:S(2)}) async-start(bf16[64,2,16384]{2,1,0:T(2,128)(2,1)} %reshape.266), calls=%async_computation | async-start | bytes 8388608 | tf_op jit(solution)/shard_map/all_to_all | solution.py:91
  116.6 0.3 all-gather.2.cloned.1.call-start
  116.9 0.0 copy-done.3
  116.9 6.2 %multiply_convert_fusion = bf16[256,8192]{1,0:T(8,128)(2,1)} fusion(f32[256,8192]{1,0:T(8,128)} %copy-done, f32[256]{0:T(256)S(1)} %pad_maximum_fusion.1), kind=kLoop, calls=%fused_computation.7 | loop fusion | flops 4194304 | bytes 12583936 | tf_op jit(solution)/shard_map/convert_element_type | solution.py:68
  123.2 6.4 %copy.35 = bf16[256,8192]{0,1:T(8,128)(2,1)} copy(bf16[256,8192]{1,0:T(8,128)(2,1)} %multiply_convert_fusion) | data formatting | bytes 8388608 | tf_op jit(solution)/shard_map/convert_element_type | solution.py:68
  129.5 3.4 gather_fusion
  132.9 0.7 bitcast_select_fusion
  133.6 0.0 all-gather.2.cloned.1.call-update
  133.6 0.0 reduce-scatter.2.cloned.1.call-start
  133.7 87.9 %all-gather.2.cloned.1.call-done = bf16[64,256,64]{1,2,0:T(8,128)(2,1)} async-done(((bf16[1,256,64]{1,2,0:T(8,128)(2,1)}), bf16[64,256,64]{1,2,0:T(8,128)(2,1)}) %all-gather.2.cloned.1.call-update) | async-done | bytes 2097168 | tf_op jit(solution)/shard_map/all_gather | solution.py:93
  221.6 2.5 reshape.250
  224.2 6.0 %copy.37 = bf16[64,2,128,64]{0,3,1,2:T(8,128)(2,1)} copy(bf16[64,2,128,64]{2,1,3,0:T(2,128)(2,1)S(1)} %reshape.250) | data formatting | bytes 4194304 | tf_op jit(solution)/shard_map/reshape | solution.py:95
  230.2 4.0 %slice_negate_fusion = (bf16[64,1,128,64]{0,3,1,2:T(8,128)(2,1)S(1)}, bf16[64,1,128,64]{0,3,1,2:T(8,128)(2,1)}) fusion(bf16[64,2,128,64]{0,3,1,2:T(8,128)(2,1)} %copy.37), kind=kLoop, calls=%fused_computation.28 | loop fusion | flops 524288 | bytes 4194304 | tf_op jit(solution)/shard_map/neg | solution.py:72
  234.2 0.0 all-to-all-done
  234.2 19.8 %reshape.267 = bf16[8192,1,256]{2,1,0:T(2,128)(2,1)} reshape(bf16[64,2,16384]{2,1,0:T(2,128)(2,1)} %all-to-all-done) | data formatting | bytes 8388608
  254.0 6.1 %copy.45 = bf16[1,256,8192]{1,2,0:T(8,128)(2,1)} copy(bf16[1,256,8192]{1,0,2:T(2,128)(2,1)} %bitcast.59) | data formatting | bytes 8388608
  260.0 6.4 %copy.34 = bf16[64,1,256,128]{3,2,0,1:T(8,128)(2,1)} copy(bf16[64,1,256,128]{2,3,0,1:T(8,128)(2,1)} %bitcast.60) | data formatting | bytes 8388608 | tf_op jit(solution)/shard_map/all_to_all | solution.py:91
  266.4 7.8 %fusion.16 = bf16[64,1,128,128]{3,0,2,1:T(8,128)(2,1)S(1)} fusion(bf16[64,2,128,64]{0,3,1,2:T(8,128)(2,1)} %copy.37, bf16[64,2,128,128]{3,2,1,0:T(8,128)(2,1)} %bitcast.61), kind=kOutput, calls=%fused_computation.26 | convolution fusion | flops 269484032 | bytes 8388608 | tf_op jit(solution)/shard_map/spfk,spfc->kfc/dot_general | solution.py:73
  274.2 0.0 copy-done.1
  274.2 0.0 copy-done.2
  274.2 4.3 %fusion.17 = bf16[64,1,128,128]{3,0,2,1:T(8,128)(2,1)S(1)} fusion(bf16[64,2,128,128]{3,2,1,0:T(8,128)(2,1)S(1)} %bitcast.62, bf16[64,1,128,64]{0,3,1,2:T(8,128)(2,1)S(1)} %copy-done.2, bf16[64,1,128,64]{0,3,1,2:T(8,128)(2,1)S(1)} %get-tuple-element.7), kind=kOutput, calls=%fused_computation.27 | convolution fusion | flops 273678336 | bytes 8388608 | tf_op jit(solution)/shard_map/spfk,spfc->kfc/dot_general | solution.py:74
  278.5 2.3 pad_maximum_fusion
  280.8 0.0 reduce-scatter.2.cloned.1.call-update
  280.9 0.1 dynamic_slice.7
  280.9 0.1 dynamic_slice.6
  281.0 0.1 compare_convert_fusion
  281.1 0.6 cosine_convert_fusion
  281.7 48.0 %reduce-scatter.2.cloned.1.call-done = bf16[16,2,128,128]{3,0,2,1:T(8,128)(2,1)} async-done(((bf16[64,2,128,128]{3,0,2,1:T(8,128)(2,1)}), bf16[16,2,128,128]{3,0,2,1:T(8,128)(2,1)}) %reduce-scatter.2.cloned.1.call-update) | async-done | bytes 1048592 | tf_op jit(solution)/shard_map/reduce_scatter | solution.py:96
  329.7 1.5 multiply_convert_fusion.3
  331.2 1.9 bitcast_multiply_fusion
  (12 shorter events, 0.1 us)
Async XLA Ops:
  7.7 13.7 %collective-permute-start = (bf16[30,8192]{1,0:T(8,128)(2,1)S(1)}, bf16[30,8192]{1,0:T(8,128)(2,1)S(1)}, u32[]{:S(2)}, u32[]{:S(2)}) collective-permute-start(bf16[30,8192]{1,0:T(8,128)(2,1)S(1)} %slice_bitcast_fusion), channel_id=1, source_target_pairs={{0,4},{4,8},{8,12},{12,16},{16,20},{20,24},{24,28},{28,32},{32,36}... | collective-permute-start | bytes 1474568 | tf_op jit(solution)/shard_map/ppermute | solution.py:20
  29.1 4.2 %copy-start = (f32[256,8192]{1,0:T(8,128)}, f32[256,8192]{1,0:T(8,128)S(1)}, u32[]{:S(2)}) copy-start(f32[256,8192]{1,0:T(8,128)S(1)} %fusion.4) | copy-start | bytes 25165828
  105.0 11.9 %copy-start.3 = (s32[64]{0:T(128)S(1)}, s32[64]{0:T(128)}, u32[]{:S(2)}) copy-start(s32[64]{0:T(128)} %param.9) | copy-start | bytes 772
  105.0 129.2 %all-to-all-start = ((bf16[64,2,16384]{2,1,0:T(2,128)(2,1)}), bf16[64,2,16384]{2,1,0:T(2,128)(2,1)}, u32[]{:S(2)}, u32[]{:S(2)}) async-start(bf16[64,2,16384]{2,1,0:T(2,128)(2,1)} %reshape.266), calls=%async_computation | async-start | bytes 8388608 | tf_op jit(solution)/shard_map/all_to_all | solution.py:91
  116.6 105.0 %all-gather.2.cloned.1.call-start = ((), (), s32[]{:S(2)}) async-start(), calls=%async_computation.2 | async-start | bytes 2129920 | tf_op jit(solution)/shard_map/all_gather | solution.py:93
  133.6 196.1 %reduce-scatter.2.cloned.1.call-start = ((), (), s32[]{:S(2)}) async-start(), calls=%async_computation.3 | async-start | bytes 5242880 | tf_op jit(solution)/shard_map/reduce_scatter | solution.py:96
  266.4 7.8 %copy-start.1 = (bf16[64,1,256,128]{3,2,0,1:T(8,128)(2,1)S(1)}, bf16[64,1,256,128]{3,2,0,1:T(8,128)(2,1)}, u32[]{:S(2)}) copy-start(bf16[64,1,256,128]{3,2,0,1:T(8,128)(2,1)} %copy.34) | copy-start | bytes 12582916
  266.4 7.8 %copy-start.2 = (bf16[64,1,128,64]{0,3,1,2:T(8,128)(2,1)S(1)}, bf16[64,1,128,64]{0,3,1,2:T(8,128)(2,1)}, u32[]{:S(2)}) copy-start(bf16[64,1,128,64]{0,3,1,2:T(8,128)(2,1)} %get-tuple-element.8) | copy-start | bytes 3145732
Sparse Core Ops, SparseCore 0:
  133.7 87.8 all-gather.1
  281.0 48.6 reduce-scatter.1
where the time goes:
time: 342 us; the launch traced here: 340 us
  waiting for transfers between devices  136 us (40%)
  local copies, waits for them, and re-layouts  77.2 us (23%)
  other arithmetic  70.9 us (21%)
  matrix products  25.8 us (8%)
  starting transfers between devices  16.4 us (5%)
  between operations  13.6 us (4%)
    all_gather x1, waiting for transfers between devices, body(): portion = lax.all_gather(picked[None], 'wide', axis=0, tiled=True)  87.9 us
    reduce_scatter x1, waiting for transfers between devices, body(): lax.psum_scatter(running.astype(jnp.bfloat16), 'narrow', scatter_dimensio...  48 us
    unnamed x1, other arithmetic  43.5 us
    unnamed x12, local copies, waits for them, and re-layouts  33.3 us
    broadcast_in_dim x1, local copies, waits for them, and re-layouts, body(): spectra[None]  17.9 us
    all_to_all x1, starting transfers between devices, body(): lax.all_to_all(spectra[None], 'wide', split_axis=2, concat_axis=0, tiled=...  11.6 us
    reshape x2, local copies, waits for them, and re-layouts, body(): running = cross_terms(portion.reshape(number, 2, F, SRC), channels)  8.58 us
    dot_general x1, matrix products, cross_terms(): jnp.einsum('spfk,spfc->kfc', sources, channels, preferred_element_type=jn...  7.79 us
  transfers between devices with their start and end apart: 4, of which 2 were waited for; matrix products, arithmetic and copies ran while one was open for 12% of the time, Pallas kernels for 0%

commit v1 on v0

v1 whole, which is shorter than its diff:
```python
import functools
import math

import jax
import jax.numpy as jnp
import numpy as np
from jax import lax
from jax.experimental import pallas as pl
from jax.experimental.pallas import tpu as pltpu
from jax.sharding import PartitionSpec as P

C = 8192
BLOCK_CH = 128
CAP = 64
Q = 2
L = 256
F = 128
K = 32
SRC = 64
NZ, NX, NC, NY = 8, 4, 2, 4
WIDE = NZ * NX * NC
HALO = 32
CHUNKS = 4
FC = F // CHUNKS
GROUP = 16
SHARE = SRC // NY
STEPS = 16
STEP_RAW = C // STEPS
STEP_CH = STEP_RAW // 2
ROW = L * Q
MESH = pl.DeviceIdType.MESH
Z_ORDER = (4, 3, 5, 2, 6, 1, 7, 0)


def dft_table():
    phases = np.arange(1, F + 1)[:, None] * np.arange(L)[None, :] % L
    angles = phases.astype(np.float32) * np.float32(2.0 * math.pi / L)
    return np.concatenate([np.cos(angles), -np.sin(angles)], axis=0).astype(jnp.bfloat16)


def lag_table():
    phases = np.arange(1, F + 1)[:, None] * (np.arange(L)[None, :] - L // 2) % L
    angles = phases.astype(np.float32) * np.float32(2.0 * math.pi / L)
    return np.stack([np.cos(angles), -np.sin(angles)], axis=0).astype(jnp.bfloat16)


def lanes(shape):
    return lax.broadcasted_iota(jnp.int32, shape, len(shape) - 1)


def paired(even, odd):
    return jnp.where(lanes(even.shape) < CAP, even, pltpu.roll(odd, CAP, 1))


def step_pair(step, z):
    plane = step // 2
    distance = jnp.int32(Z_ORDER[-1])
    for i, d in enumerate(Z_ORDER[:-1]):
        distance = jnp.where(plane == i, jnp.int32(d), distance)
    return lax.rem(z + distance, NZ) * NX + lax.rem(step, 2) * 2


def spectra_kernel(
    raw, first_row, dft, weights, source_row, source_col, out,
    samples, edge, edge_out, edge_in, taps, decimated, level_acc, source_acc,
    outgoing, incoming, sources, chan_t, source_t, cross, parts,
    raw_sem, edge_sem, halo_send, halo_recv, send_sem, recv_sem,
    gather_send, gather_recv, y_send, y_recv,
):
    w = lax.axis_index("wide")
    y = lax.axis_index("narrow")
    z, x, core = w // (NX * NC), lax.rem(w // NC, NX), lax.rem(w, NC)

    edge_copy = pltpu.make_async_copy(raw.at[0, pl.ds(ROW - HALO, HALO)], edge, edge_sem)
    edge_copy.start()

    def raw_copy(step):
        at = pl.multiple_of(step_pair(step, z) * 2 * BLOCK_CH, STEP_RAW)
        return pltpu.make_async_copy(
            raw.at[0, :, pl.ds(at, STEP_RAW)], samples.at[step], raw_sem.at[step]
        )

    @pl.loop(0, STEPS)
    def _(step):
        raw_copy(step).start()

    barrier = pltpu.get_barrier_semaphore()

    @pl.loop(1, WIDE)
    def _(t):
        pl.semaphore_signal(
            barrier, inc=1, device_id=(lax.rem(w + t, WIDE), y), device_id_type=MESH
        )

    for t in range(1, NY):
        pl.semaphore_signal(
            barrier, inc=1, device_id=(w, lax.rem(y + t, NY)), device_id_type=MESH
        )

    circular = pltpu.roll(
        jnp.broadcast_to(first_row[0:1, :], (L, ROW)), 0, 1, stride=Q, stride_axis=0
    )
    rows = lax.broadcasted_iota(jnp.int32, (L, ROW), 0)
    inside = lanes((L, ROW)) <= Q * rows + 1
    taps[...] = jnp.where(inside, circular, 0.0).astype(jnp.bfloat16)
    halo_taps = jnp.where(inside[:16], 0.0, circular[:16])[:, ROW - BLOCK_CH :]
    halo_taps = pltpu.roll(jnp.where(w == 0, 0.0, halo_taps), HALO, 1)[:, :HALO]
    halo_taps = halo_taps.astype(jnp.bfloat16)

    edge_copy.wait()
    for b in range(C // BLOCK_CH // 2):
        at = 2 * b * BLOCK_CH
        pair = edge[:, at : at + 2 * BLOCK_CH].astype(jnp.float32)
        edge_out[:, b * BLOCK_CH : (b + 1) * BLOCK_CH] = paired(
            pair[:, :BLOCK_CH], pair[:, BLOCK_CH:]
        ).astype(jnp.bfloat16)

    pl.semaphore_wait(barrier, WIDE - 1 + NY - 1)
    halo = pltpu.make_async_remote_copy(
        src_ref=edge_out,
        dst_ref=edge_in,
        send_sem=halo_send,
        recv_sem=halo_recv,
        device_id=(lax.rem(w + 1, WIDE), y),
        device_id_type=MESH,
    )
    halo.start()

    level_acc[...] = jnp.zeros_like(level_acc)
    source_acc[...] = jnp.zeros_like(source_acc)

    @pl.loop(0, STEPS)
    def _(step):
        raw_copy(step).wait()
        d = jnp.dot(taps[...], samples[step], preferred_element_type=jnp.float32)
        for p in range(2):
            at = 2 * p * BLOCK_CH
            decimated[step, :, p * BLOCK_CH : (p + 1) * BLOCK_CH] = paired(
                d[:, at : at + BLOCK_CH], d[:, at + BLOCK_CH : at + 2 * BLOCK_CH]
            )

    halo.wait()

    def send(chunk, dest):
        return pltpu.make_async_remote_copy(
            src_ref=outgoing.at[chunk, dest],
            dst_ref=incoming.at[chunk, w],
            send_sem=send_sem.at[chunk],
            recv_sem=recv_sem.at[chunk],
            device_id=(dest, y),
            device_id_type=MESH,
        )

    def own(chunk):
        return pltpu.make_async_copy(
            outgoing.at[chunk, w], incoming.at[chunk, w], recv_sem.at[chunk]
        )

    def start_send(chunk, dest):
        @pl.when(dest != w)
        def _():
            send(chunk, dest).start()

        @pl.when(dest == w)
        def _():
            own(chunk).start()

    @pl.loop(0, STEPS)
    def _(step):
        first = step_pair(step, z)
        at = pl.multiple_of(first * BLOCK_CH, STEP_CH)
        head = jnp.dot(
            halo_taps,
            edge_in[:, pl.ds(at, STEP_CH)],
            preferred_element_type=jnp.float32,
        )
        d = decimated[step]
        d = jnp.concatenate([d[:16] + head, d[16:]], axis=0)
        scaling = lax.rsqrt(jnp.sum(d * d, axis=0, keepdims=True) * (1.0 / L) + 1e-06)
        normed = (d * scaling).astype(jnp.bfloat16)
        spectra = jnp.dot(dft[...], normed, preferred_element_type=jnp.float32)
        total = level_acc[...]
        for p in range(2):
            pair = first + p
            re = spectra[:F, p * BLOCK_CH : (p + 1) * BLOCK_CH]
            im = spectra[F:, p * BLOCK_CH : (p + 1) * BLOCK_CH]
            total = total + (re * re + im * im) * weights[pl.ds(pair, 1), :]
            low = lanes(re.shape) < CAP
            blocks = (
                jnp.where(low, re, pltpu.roll(im, CAP, 1)).astype(jnp.bfloat16),
                jnp.where(low, pltpu.roll(re, CAP, 1), im).astype(jnp.bfloat16),
            )
            for c in range(NC):
                for chunk in range(CHUNKS):
                    outgoing[chunk, 2 * pair + c] = blocks[c][chunk * FC : (chunk + 1) * FC]
        level_acc[...] = total
        for p in range(2):
            for c in range(NC):
                start_send(0, 2 * (first + p) + c)
        slots = lax.broadcasted_iota(jnp.int32, (STEP_CH, BLOCK_CH), 0)
        ids = (2 * first + slots // CAP) * BLOCK_CH + lax.rem(slots, CAP)
        chosen = (ids == source_row[...]).astype(jnp.float32).astype(jnp.bfloat16)
        source_acc[...] += jnp.dot(
            spectra.astype(jnp.bfloat16), chosen, preferred_element_type=jnp.float32
        )

    levels = jnp.sum(level_acc[...], axis=1, keepdims=True) / jnp.sum(weights[...]) + 1e-06
    picked = source_acc[...]
    picked = jnp.where(lanes((F, BLOCK_CH)) < SRC, picked[:F], picked[F:])
    sources[z, x, core] = (picked / levels).astype(jnp.bfloat16)

    def gather(phase, view, device):
        return pltpu.make_async_remote_copy(
            src_ref=view,
            dst_ref=view,
            send_sem=gather_send.at[phase],
            recv_sem=gather_recv.at[phase],
            device_id=(device, y),
            device_id_type=MESH,
        )

    def arrived(view, sem):
        pltpu.make_async_copy(view, view, sem).wait()

    def send_rest(chunk):
        @pl.loop(0, WIDE)
        def _(t):
            start_send(chunk, lax.rem(w + WIDE // 2 + t, WIDE))

    for t in range(1, NZ):
        to = (lax.rem(z + t, NZ) * NX + x) * NC + core
        gather(0, sources.at[z, x, core], to).start()
    send_rest(1)
    arrived(sources.at[pl.ds(0, NZ - 1), x, core], gather_recv.at[0])
    for t in range(1, NX):
        to = (z * NX + lax.rem(x + t, NX)) * NC + core
        gather(1, sources.at[:, x, core], to).start()
    send_rest(2)
    arrived(sources.at[:, pl.ds(0, NX - 1), core], gather_recv.at[1])
    gather(2, sources.at[:, :, core], w + 1 - 2 * core).start()
    send_rest(3)
    arrived(sources.at[:, :, 1 - core], gather_recv.at[2])

    def y_copy(chunk, to):
        return pltpu.make_async_remote_copy(
            src_ref=cross.at[chunk, to],
            dst_ref=parts.at[chunk, y],
            send_sem=y_send.at[chunk],
            recv_sem=y_recv.at[chunk],
            device_id=(w, to),
            device_id_type=MESH,
        )

    sign = jnp.where(lanes((SRC, BLOCK_CH)) < CAP, 1.0, -1.0)

    def cross_chunk(chunk):
        arrived(incoming.at[chunk], recv_sem.at[chunk])

        @pl.loop(0, FC // GROUP)
        def _(g):
            at = pl.multiple_of(g * GROUP, GROUP)
            full = pl.multiple_of(chunk * FC + g * GROUP, GROUP)
            for q in range(WIDE // GROUP):
                held = incoming[chunk, q * GROUP : (q + 1) * GROUP, pl.ds(at, GROUP), :]
                chan_t[:, q * GROUP : (q + 1) * GROUP, :] = jnp.swapaxes(held, 0, 1)
                held = sources[2 * q : 2 * q + 2, :, :, pl.ds(full, GROUP), :]
                held = held.reshape(GROUP, GROUP, BLOCK_CH)
                source_t[:, q * GROUP : (q + 1) * GROUP, :] = jnp.swapaxes(held, 0, 1)
            for f in range(GROUP):
                product = lax.dot_general(
                    source_t[f], chan_t[f], (((0,), (0,)), ((), ())),
                    preferred_element_type=jnp.float32,
                )
                both = product[:SRC] + sign * pltpu.roll(product[SRC:], CAP, 1)
                both = both.astype(jnp.bfloat16)
                for k in range(NY):
                    cross[chunk, k, at + f] = both[k * SHARE : (k + 1) * SHARE]

        for t in range(1, NY):
            y_copy(chunk, lax.rem(y + t, NY)).start()
        pltpu.make_async_copy(cross.at[chunk, y], parts.at[chunk, y], y_recv.at[chunk]).start()

    lane = lanes((1, BLOCK_CH))
    alive = weights[pl.ds(w // 2, 1), :]
    turned = pltpu.roll(alive, CAP, 1)
    alive = jnp.where((lane < CAP) == (core == 0), alive, turned)
    own_ids = source_col[pl.ds(pl.multiple_of(y * SHARE, SHARE), SHARE), :]
    distinct = (w * BLOCK_CH + lax.rem(lane, CAP)) != own_ids
    keep = jnp.where(distinct, alive, 0.0)

    def sum_chunk(chunk):
        arrived(parts.at[chunk], y_recv.at[chunk])

        @pl.loop(0, FC)
        def _(f):
            total = parts[chunk, 0, f].astype(jnp.float32)
            for n in range(1, NY):
                total = total + parts[chunk, n, f].astype(jnp.float32)
            out[chunk * FC + f] = (total * keep).astype(jnp.bfloat16)

    for chunk in range(CHUNKS):
        cross_chunk(chunk)
        if chunk >= 1:
            sum_chunk(chunk - 1)
    sum_chunk(CHUNKS - 1)

    for chunk in range(CHUNKS):
        arrived(outgoing.at[chunk, pl.ds(0, WIDE - 1)], send_sem.at[chunk])
        arrived(cross.at[chunk, pl.ds(0, NY - 1)], y_send.at[chunk])
    arrived(sources.at[pl.ds(0, NZ - 1), x, core], gather_send.at[0])
    arrived(sources.at[:, pl.ds(0, NX - 1), core], gather_send.at[1])
    arrived(sources.at[:, :, core], gather_send.at[2])


def masked_spectra(raw, first_row, dft, weights, source_row, source_col):
    bf16, f32 = jnp.bfloat16, jnp.float32
    dma = pltpu.SemaphoreType.DMA
    vmem = pl.BlockSpec(memory_space=pltpu.VMEM)
    return pl.pallas_call(
        spectra_kernel,
        out_shape=jax.ShapeDtypeStruct((F, SHARE, BLOCK_CH), bf16),
        in_specs=[pl.BlockSpec(memory_space=pl.ANY)] + [vmem] * 5,
        out_specs=vmem,
        scratch_shapes=[
            pltpu.VMEM((STEPS, ROW, STEP_RAW), bf16),
            pltpu.VMEM((HALO, C), bf16),
            pltpu.VMEM((HALO, C // 2), bf16),
            pltpu.VMEM((HALO, C // 2), bf16),
            pltpu.VMEM((L, ROW), bf16),
            pltpu.VMEM((STEPS, L, STEP_CH), f32),
            pltpu.VMEM((F, BLOCK_CH), f32),
            pltpu.VMEM((2 * F, BLOCK_CH), f32),
            pltpu.VMEM((CHUNKS, WIDE, FC, BLOCK_CH), bf16),
            pltpu.VMEM((CHUNKS, WIDE, FC, BLOCK_CH), bf16),
            pltpu.VMEM((NZ, NX, NC, F, BLOCK_CH), bf16),
            pltpu.VMEM((GROUP, WIDE, BLOCK_CH), bf16),
            pltpu.VMEM((GROUP, WIDE, BLOCK_CH), bf16),
            pltpu.VMEM((CHUNKS, NY, FC, SHARE, BLOCK_CH), bf16),
            pltpu.VMEM((CHUNKS, NY, FC, SHARE, BLOCK_CH), bf16),
            dma((STEPS,)),
            dma,
            dma,
            dma,
            dma((CHUNKS,)),
            dma((CHUNKS,)),
            dma((3,)),
            dma((3,)),
            dma((CHUNKS,)),
            dma((CHUNKS,)),
        ],
        compiler_params=pltpu.CompilerParams(
            collective_id=0, has_side_effects=True, vmem_limit_bytes=48 << 20
        ),
        name="masked_spectra",
    )(raw, first_row, dft, weights, source_row, source_col)


def lag_kernel(masked, table, out, by_source):
    step = pl.program_id(0)

    @pl.when(step == 0)
    def _():
        by_source[...] = jnp.swapaxes(masked[...], 0, 1)

    factor = 1.0 / math.sqrt(WIDE * NY * F)
    for k in range(out.shape[0]):
        turned = by_source[step * out.shape[0] + k].T
        out[k, :CAP] = factor * (
            jnp.dot(turned[:CAP], table[0], preferred_element_type=jnp.float32)
            + jnp.dot(turned[CAP:], table[1], preferred_element_type=jnp.float32)
        )
        out[k, CAP:] = jnp.zeros((BLOCK_CH - CAP, L), jnp.float32)


def correlations(masked, table):
    part = 4
    return pl.pallas_call(
        lag_kernel,
        grid=(SHARE // part,),
        out_shape=jax.ShapeDtypeStruct((SHARE, BLOCK_CH, L), jnp.float32),
        in_specs=[
            pl.BlockSpec((F, SHARE, BLOCK_CH), lambda i: (0, 0, 0)),
            pl.BlockSpec((2, F, L), lambda i: (0, 0, 0)),
        ],
        out_specs=pl.BlockSpec((part, BLOCK_CH, L), lambda i: (i, 0, 0)),
        scratch_shapes=[pltpu.VMEM((SHARE, F, BLOCK_CH), jnp.bfloat16)],
        compiler_params=pltpu.CompilerParams(vmem_limit_bytes=16 << 20),
        name="correlations",
    )(masked, table)


def body(raw_record, filter_taps, health_mask, counts, source_index):
    taps = filter_taps.astype(jnp.float32)
    first_row = jnp.concatenate(
        [taps[1::-1], jnp.zeros((ROW - K,), jnp.float32), taps[:1:-1]]
    )
    first_row = jnp.broadcast_to(first_row[None, :], (8, ROW))
    slots = jnp.arange(CAP, dtype=jnp.int32)[None, :]
    living = health_mask.reshape(C // BLOCK_CH, BLOCK_CH)[:, :CAP] * (counts[:, None] > slots)
    weights = living.astype(jnp.float32).reshape(WIDE // 2, 2 * CAP)
    source_row = jnp.concatenate([source_index, source_index])[None, :]
    source_col = jnp.broadcast_to(source_index[:, None], (SRC, BLOCK_CH))
    masked = masked_spectra(
        raw_record, first_row, jnp.asarray(dft_table()), weights, source_row, source_col
    )
    return correlations(masked, jnp.asarray(lag_table()))


def solution(mesh):
    placed = (P("narrow", "wide", None), P(), P(), P(), P())
    return jax.shard_map(
        body, mesh=mesh, in_specs=placed, out_specs=P("narrow", "wide", None), check_vma=False
    )
```

time: 342 us -> 98.1 us (0.29)
  waiting for transfers between devices: 136 us -> 0 us
  Pallas kernels: 0 us -> 92.8 us
  local copies, waits for them, and re-layouts: 77.2 us -> 3.33 us
  other arithmetic: 70.9 us -> 1.72 us
  matrix products: 25.8 us -> 0 us
  starting transfers between devices: 16.4 us -> 0 us
  between operations: 13.6 us -> 0.02 us
    pallas_call x0 -> x2, Pallas kernels: none -> 92.8 us  [the longest x1 90.2 us: masked_spectra(): pl.pallas_call(spectra_kernel, out_shape=jax.ShapeDtypeStruct((F, SHARE,...]
    all_gather x1 -> x0, waiting for transfers between devices: 87.9 us -> none  [body(): portion = lax.all_gather(picked[None], 'wide', axis=0, tiled=True)]
    reduce_scatter x1 -> x0, waiting for transfers between devices: 48 us -> none  [body(): lax.psum_scatter(running.astype(jnp.bfloat16), 'narrow', scatter_dimensio...]
    unnamed x1 -> x0, other arithmetic: 43.5 us -> none
    unnamed x12 -> x4, local copies, waits for them, and re-layouts: 33.3 us -> 0.91 us
    dot_general x6 -> x0, matrix products: 25.8 us -> none  [the longest x1 7.79 us: cross_terms(): jnp.einsum('spfk,spfc->kfc', sources, channels, preferred_element_type=jn...]
    broadcast_in_dim x1 -> x3, local copies, waits for them, and re-layouts: 17.9 us -> 0.74 us  [the longest x1 0.73 us: body(): source_col = jnp.broadcast_to(source_index[:, None], (SRC, BLOCK_CH))]
    all_to_all x1 -> x0, starting transfers between devices: 11.6 us -> none  [body(): lax.all_to_all(spectra[None], 'wide', split_axis=2, concat_axis=0, tiled=...]
  transfers between devices with their start and end apart: 4 -> 0, of which waited for: 2 -> 0; matrix products, arithmetic and copies ran while one was open for 12% -> 0% of each run, Pallas kernels for 0% -> 0%
where the time goes in v1:
time: 98.1 us; the launch traced here: 97.9 us
  Pallas kernels  92.8 us (95%)
  local copies, waits for them, and re-layouts  3.33 us (3%)
  other arithmetic  1.72 us (2%)
    pallas_call x1, Pallas kernels, masked_spectra(): pl.pallas_call(spectra_kernel, out_shape=jax.ShapeDtypeStruct((F, SHARE,...  90.2 us
    pallas_call x1, Pallas kernels, correlations(): pl.pallas_call(lag_kernel, grid=(SHARE // part,), out_shape=jax.ShapeDtyp...  2.57 us

profile of v1, /device:TPU:1, one launch (start us, length us, event | category | flops | bytes accessed | tf_op | source)
XLA Modules:
  0.0 97.9 jit_solution(9199297630326319441)
XLA Ops:
  0.0 0.0 copy-start.1
  0.0 0.8 slice.10
  0.8 0.1 rev.7
  0.9 0.7 slice.9
  1.5 0.1 rev.6
  1.6 0.8 add_bitcast_fusion.source_row
  2.4 0.1 pad_maximum_fusion
  2.5 0.8 fusion
  3.3 0.1 reshape.10.weights
  3.4 0.7 broadcast_in_dim.11.source_col
  4.1 0.0 copy-start
  4.1 0.9 copy-done
  5.1 90.2 %masked_spectra.1.masked = bf16[128,16,128]{2,1,0:T(8,128)(2,1)S(1)} custom-call(bf16[1,512,8192]{2,1,0:T(8,128)(2,1)} %raw.1, f32[8,512]{1,0:T(8,128)S(1)} %broadcast_in_dim.9.first_row, bf16[256,256]{1,0:T(8,128)(2,1)S(1)} %copy-done, f32[32,128]{1,0:T(8,128)S(1)} %reshape.10.weights, s32[1,128]{1,0:T(1,128)S(1)} %add_bitcast_fusion.source_row, ...), custom_call_target="tpu_custom_call" | custom-call | tf_op jit(solution)/shard_map/masked_spectra/pallas_call | solution.py:319
  95.3 0.0 copy-done.1
  95.3 2.6 %correlations.1 = f32[16,128,256]{2,1,0:T(8,128)} custom-call(bf16[128,16,128]{2,1,0:T(8,128)(2,1)S(1)} %masked_spectra.1.masked, bf16[2,128,256]{2,1,0:T(8,128)(2,1)S(1)} %copy-done.1), custom_call_target="tpu_custom_call" | custom-call | tf_op jit(solution)/shard_map/correlations/pallas_call | solution.py:377
  (2 shorter events, 0.0 us)
Async XLA Ops:
  0.0 95.3 %copy-start.1 = (bf16[2,128,256]{2,1,0:T(8,128)(2,1)S(1)}, bf16[2,128,256]{2,1,0:T(8,128)(2,1)}, u32[]{:S(2)}) copy-start(bf16[2,128,256]{2,1,0:T(8,128)(2,1)} %constant.9.clone.table) | copy-start | bytes 393220
  4.1 0.9 copy-start

commit v2 on v1

v2 whole, which is shorter than its diff:
```python
import functools
import math

import jax
import jax.numpy as jnp
import numpy as np
from jax import lax
from jax.experimental import pallas as pl
from jax.experimental.pallas import tpu as pltpu
from jax.sharding import PartitionSpec as P

C = 8192
BLOCK_CH = 128
CAP = 64
Q = 2
L = 256
F = 128
K = 32
SRC = 64
NZ, NX, NC, NY = 8, 4, 2, 4
WIDE = NZ * NX * NC
HALO = 32
NXC = NX * NC
PLANE = NXC * NY
FC = F // NY
GROUP = 16
SHARE = SRC // NY
STEPS = NZ
STEP_RAW = C // STEPS
STEP_CH = STEP_RAW // 2
ROW = L * Q
MESH = pl.DeviceIdType.MESH
Z_ORDER = (4, 3, 5, 2, 6, 1, 7, 0)
GROUPS = ((0, 1), (1, 2), (3, 2), (5, 2), (7, 1))
HOPS = 7
TAIL = 8
TAILS = FC // TAIL


def dft_table():
    phases = np.arange(1, F + 1)[:, None] * np.arange(L)[None, :] % L
    angles = phases.astype(np.float32) * np.float32(2.0 * math.pi / L)
    return np.concatenate([np.cos(angles), -np.sin(angles)], axis=0).astype(jnp.bfloat16)


def lag_table():
    phases = np.arange(1, F + 1)[:, None] * (np.arange(L)[None, :] - L // 2) % L
    angles = phases.astype(np.float32) * np.float32(2.0 * math.pi / L)
    return np.stack([np.cos(angles), -np.sin(angles)], axis=0).astype(jnp.bfloat16)


def lanes(shape):
    return lax.broadcasted_iota(jnp.int32, shape, len(shape) - 1)


def paired(even, odd):
    return jnp.where(lanes(even.shape) < CAP, even, pltpu.roll(odd, CAP, 1))


def step_plane(step, z):
    distance = jnp.int32(Z_ORDER[-1])
    for i, d in enumerate(Z_ORDER[:-1]):
        distance = jnp.where(step == i, jnp.int32(d), distance)
    return lax.rem(z + distance, NZ)


def spectra_kernel(
    raw, filter_taps, dft_hbm, health_hbm, counts_hbm, index_hbm, out,
    dft, health, counts, source_index, small_sem,
    samples, edge, edge_out, edge_in, taps, tap_row, decimated, level_acc, weight_acc, source_acc,
    outgoing, incoming, source_out, source_in, source_t, chan_t, sums, right_in, left_in,
    masked, quarters,
    raw_sem, edge_sem, halo_send, halo_recv, send_sem, recv_sem, source_send, source_recv,
    right_send, right_recv, left_send, left_recv, y_send, y_recv,
):
    w = lax.axis_index("wide")
    y = lax.axis_index("narrow")
    z, xc = w // NXC, lax.rem(w, NXC)
    me = xc * NY + y

    def peer(t):
        other = lax.rem(me + t, PLANE)
        return other // NY, lax.rem(other, NY)

    edge_copy = pltpu.make_async_copy(raw.at[0, pl.ds(ROW - HALO, HALO)], edge, edge_sem)
    edge_copy.start()
    small = [
        pltpu.make_async_copy(src, dst, small_sem.at[i])
        for i, (src, dst) in enumerate(
            (
                (index_hbm, source_index),
                (counts_hbm, counts),
                (health_hbm, health),
                (dft_hbm, dft),
            )
        )
    ]
    for copy in small:
        copy.start()

    def raw_copy(step):
        at = pl.multiple_of(step_plane(step, z) * STEP_RAW, STEP_RAW)
        return pltpu.make_async_copy(
            raw.at[0, :, pl.ds(at, STEP_RAW)], samples.at[step], raw_sem.at[step]
        )

    @pl.loop(0, STEPS)
    def _(step):
        raw_copy(step).start()

    barrier = pltpu.get_barrier_semaphore()

    def greet(wide, narrow):
        pl.semaphore_signal(barrier, inc=1, device_id=(wide, narrow), device_id_type=MESH)

    z_right, z_left = lax.rem(w + NXC, WIDE), lax.rem(w + WIDE - NXC, WIDE)
    after, before = lax.rem(w + 1, WIDE), lax.rem(w + WIDE - 1, WIDE)
    for wide in (after, before, z_right, z_left):
        greet(wide, y)

    @pl.loop(1, PLANE)
    def _(t):
        to_xc, to_y = peer(t)
        greet(z * NXC + to_xc, to_y)

    edge_copy.wait()
    for b in range(C // BLOCK_CH // 2):
        at = 2 * b * BLOCK_CH
        pair = edge[:, at : at + 2 * BLOCK_CH].astype(jnp.float32)
        edge_out[:, b * BLOCK_CH : (b + 1) * BLOCK_CH] = paired(
            pair[:, :BLOCK_CH], pair[:, BLOCK_CH:]
        ).astype(jnp.bfloat16)

    pl.semaphore_wait(barrier, PLANE - 1 + 4)

    def halo(plane):
        columns = pl.ds(pl.multiple_of(plane * STEP_CH, STEP_CH), STEP_CH)
        return pltpu.make_async_remote_copy(
            src_ref=edge_out.at[:, columns],
            dst_ref=edge_in.at[:, columns],
            send_sem=halo_send.at[plane],
            recv_sem=halo_recv.at[plane],
            device_id=(after, y),
            device_id_type=MESH,
        )

    @pl.loop(0, STEPS)
    def _(step):
        halo(step_plane(step, z)).start()

    tap_row[...] = jnp.zeros_like(tap_row)
    tap_row[0:1, :K] = filter_taps[...].astype(jnp.float32)
    tap_ids = lax.broadcasted_iota(jnp.int32, (BLOCK_CH, ROW), 0)
    place = (lanes((BLOCK_CH, ROW)) + tap_ids == 1) | (lanes((BLOCK_CH, ROW)) + tap_ids == ROW + 1)
    first_row = jnp.dot(
        tap_row[...].astype(jnp.bfloat16),
        jnp.where(place, 1.0, 0.0).astype(jnp.bfloat16),
        preferred_element_type=jnp.float32,
    )
    circular = pltpu.roll(
        jnp.broadcast_to(first_row[0:1, :], (L, ROW)), 0, 1, stride=Q, stride_axis=0
    )
    rows = lax.broadcasted_iota(jnp.int32, (L, ROW), 0)
    inside = lanes((L, ROW)) <= Q * rows + 1
    taps[...] = jnp.where(inside, circular, 0.0).astype(jnp.bfloat16)
    halo_taps = jnp.where(inside[:16], 0.0, circular[:16])[:, ROW - BLOCK_CH :]
    halo_taps = pltpu.roll(jnp.where(w == 0, 0.0, halo_taps), HALO, 1)[:, :HALO]
    halo_taps = halo_taps.astype(jnp.bfloat16)

    lane = lanes((1, BLOCK_CH))
    slot_lane = lax.rem(lane, CAP)
    for copy in small:
        copy.wait()
    source_row = jnp.zeros((1, BLOCK_CH), jnp.int32)
    for k in range(SRC):
        source_row = jnp.where(slot_lane == k, source_index[k], source_row)

    level_acc[...] = jnp.zeros_like(level_acc)
    weight_acc[...] = jnp.zeros_like(weight_acc)
    source_acc[...] = jnp.zeros_like(source_acc)

    @pl.loop(0, STEPS)
    def _(step):
        raw_copy(step).wait()
        d = jnp.dot(taps[...], samples[step], preferred_element_type=jnp.float32)
        for p in range(NX):
            at = 2 * p * BLOCK_CH
            decimated[step, :, p * BLOCK_CH : (p + 1) * BLOCK_CH] = paired(
                d[:, at : at + BLOCK_CH], d[:, at + BLOCK_CH : at + 2 * BLOCK_CH]
            )

    def spectra_step(step):
        plane = step_plane(step, z)
        first = plane * NX
        at = pl.multiple_of(plane * STEP_CH, STEP_CH)
        halo(plane).wait_recv()
        head = jnp.dot(
            halo_taps, edge_in[:, pl.ds(at, STEP_CH)], preferred_element_type=jnp.float32
        )
        d = decimated[step]
        d = jnp.concatenate([d[:16] + head, d[16:]], axis=0)
        scaling = lax.rsqrt(jnp.sum(d * d, axis=0, keepdims=True) * (1.0 / L) + 1e-06)
        normed = (d * scaling).astype(jnp.bfloat16)
        spectra = jnp.dot(dft[...], normed, preferred_element_type=jnp.float32)
        total = level_acc[...]
        for p in range(NX):
            pair = first + p
            re = spectra[:F, p * BLOCK_CH : (p + 1) * BLOCK_CH]
            im = spectra[F:, p * BLOCK_CH : (p + 1) * BLOCK_CH]
            flags = paired(health[pl.ds(2 * pair, 1), :], health[pl.ds(2 * pair + 1, 1), :])
            count = jnp.where(lane < CAP, counts[2 * pair], counts[2 * pair + 1])
            weights = jnp.where(slot_lane < count, flags, 0).astype(jnp.float32)
            weight_acc[...] += weights
            total = total + (re * re + im * im) * weights
            low = lanes(re.shape) < CAP
            outgoing[step, 2 * p] = jnp.where(low, re, pltpu.roll(im, CAP, 1)).astype(jnp.bfloat16)
            outgoing[step, 2 * p + 1] = jnp.where(low, pltpu.roll(re, CAP, 1), im).astype(
                jnp.bfloat16
            )
        level_acc[...] = total
        slots = lax.broadcasted_iota(jnp.int32, (STEP_CH, BLOCK_CH), 0)
        ids = (2 * first + slots // CAP) * BLOCK_CH + lax.rem(slots, CAP)
        chosen = (ids == source_row).astype(jnp.float32).astype(jnp.bfloat16)
        source_acc[...] += jnp.dot(
            spectra.astype(jnp.bfloat16), chosen, preferred_element_type=jnp.float32
        )

    def bins(to_y):
        return pl.ds(pl.multiple_of(to_y * FC, FC), FC)

    def send_group(group):
        slots = pl.ds(*GROUPS[group])

        @pl.loop(1, PLANE)
        def _(t):
            to_xc, to_y = peer(t)
            pltpu.make_async_remote_copy(
                src_ref=outgoing.at[slots, to_xc, bins(to_y)],
                dst_ref=incoming.at[slots, me],
                send_sem=send_sem.at[group],
                recv_sem=recv_sem.at[group],
                device_id=(z * NXC + to_xc, to_y),
                device_id_type=MESH,
            ).start()

        pltpu.make_async_copy(
            outgoing.at[slots, xc, bins(y)], incoming.at[slots, me], recv_sem.at[group]
        ).start()

    def arrived(view, sem):
        pltpu.make_async_copy(view, view, sem).wait()

    spectra_step(0)
    send_group(0)

    @pl.loop(1, STEPS)
    def _(step):
        spectra_step(step)

    levels = jnp.sum(level_acc[...], axis=1, keepdims=True) / jnp.sum(weight_acc[...]) + 1e-06
    picked = source_acc[...]
    picked = jnp.where(lanes((F, BLOCK_CH)) < SRC, picked[:F], picked[F:])
    source_out[...] = (picked / levels).astype(jnp.bfloat16)

    @pl.loop(1, PLANE)
    def _(t):
        to_xc, to_y = peer(t)
        pltpu.make_async_remote_copy(
            src_ref=source_out.at[bins(to_y)],
            dst_ref=source_in.at[me],
            send_sem=source_send,
            recv_sem=source_recv,
            device_id=(z * NXC + to_xc, to_y),
            device_id_type=MESH,
        ).start()

    pltpu.make_async_copy(source_out.at[bins(y)], source_in.at[me], source_recv).start()
    send_group(1)

    def by_bin(held, turned):
        for f in range(FC // GROUP):
            for q in range(PLANE // GROUP):
                turned[f * GROUP : (f + 1) * GROUP, q * GROUP : (q + 1) * GROUP, :] = jnp.swapaxes(
                    held[q * GROUP : (q + 1) * GROUP, f * GROUP : (f + 1) * GROUP, :], 0, 1
                )

    arrived(source_in, source_recv)
    by_bin(source_in, source_t)
    sign = jnp.where(lanes((SRC, BLOCK_CH)) < CAP, 1.0, -1.0)

    def cross_slots(group):
        first, number = GROUPS[group]
        arrived(incoming.at[pl.ds(first, number)], recv_sem.at[group])
        for slot in range(first, first + number):
            by_bin(incoming.at[slot], chan_t)

            @pl.loop(0, FC // 8)
            def _(g, slot=slot):
                for i in range(8):
                    f = g * 8 + i
                    product = lax.dot_general(
                        source_t[f], chan_t[f], (((0,), (0,)), ((), ())),
                        preferred_element_type=jnp.float32,
                    )
                    both = product[:SRC] + sign * pltpu.roll(product[SRC:], CAP, 1)
                    both = both.astype(jnp.bfloat16)
                    for k in range(NY):
                        sums[slot, k, f] = both[k * SHARE : (k + 1) * SHARE]

    right = ((0, 0), (1, 1), (1, 0), (3, 1), (3, 0), (5, 1), (5, 0))
    left = ((0, 1), (2, 0), (2, 1), (4, 0), (4, 1), (6, 0), (6, 1))

    def half(slot, part):
        return sums.at[slot, pl.ds(2 * part, 2)]

    def tail(ref, i):
        return ref.at[:, pl.ds(i * TAIL, TAIL)]

    def add_in(slot, part, landed):
        @pl.loop(0, FC)
        def _(f):
            for k in range(2):
                both = sums[slot, 2 * part + k, f].astype(jnp.float32)
                both = both + landed[k, f].astype(jnp.float32)
                sums[slot, 2 * part + k, f] = both.astype(jnp.bfloat16)

    def forward(m):
        for route, landed, sends, recvs, to in (
            (right, right_in, right_send, right_recv, z_right),
            (left, left_in, left_send, left_recv, z_left),
        ):
            slot, part = route[m]
            if m >= 2:
                arrived(landed.at[m - 2], recvs.at[m - 2])
                add_in(slot, part, landed.at[m - 2])
            if m < HOPS - 1:
                pieces = [(half(slot, part), landed.at[m], m)]
            else:
                pieces = [
                    (tail(half(slot, part), i), tail(landed.at[m], i), m + i) for i in range(TAILS)
                ]
            for src, dst, sem in pieces:
                pltpu.make_async_remote_copy(
                    src_ref=src,
                    dst_ref=dst,
                    send_sem=sends.at[sem],
                    recv_sem=recvs.at[sem],
                    device_id=(to, y),
                    device_id_type=MESH,
                ).start()

    cross_slots(0)
    forward(0)
    send_group(2)
    cross_slots(1)
    forward(1)
    forward(2)
    send_group(3)
    send_group(4)
    cross_slots(2)
    forward(3)
    forward(4)
    cross_slots(3)
    forward(5)
    forward(6)
    cross_slots(4)

    alive = jnp.where(slot_lane < counts[w], health[pl.ds(w, 1), :], 0)
    alive = jnp.where(lane < CAP, alive, pltpu.roll(alive, CAP, 1)).astype(jnp.float32)
    own_ids = w * BLOCK_CH + slot_lane
    row_ids = lax.broadcasted_iota(jnp.int32, (SHARE, BLOCK_CH), 0)
    keeps = []
    for k in range(NY):
        ids = jnp.zeros((SHARE, BLOCK_CH), jnp.int32)
        for i in range(SHARE):
            ids = jnp.where(row_ids == i, source_index[k * SHARE + i], ids)
        keeps.append(jnp.where(ids != own_ids, alive, 0.0))
    last = HOPS - 1
    arrived(right_in.at[last - 1], right_recv.at[last - 1])
    arrived(left_in.at[last - 1], left_recv.at[last - 1])
    for i in range(TAILS):
        arrived(tail(right_in.at[last], i), right_recv.at[last + i])
        arrived(tail(left_in.at[last], i), left_recv.at[last + i])

        @pl.loop(i * TAIL, (i + 1) * TAIL)
        def _(f):
            for k in range(NY):
                total = sums[NZ - 1, k, f].astype(jnp.float32)
                from_right = right_in[last - k // 2, k % 2, f]
                from_left = left_in[last - 1 + k // 2, k % 2, f]
                total = total + from_right.astype(jnp.float32) + from_left.astype(jnp.float32)
                masked[k, f] = (total * keeps[k]).astype(jnp.bfloat16)

        part = pl.ds(i * TAIL, TAIL)
        for t in range(1, NY):
            to = lax.rem(y + t, NY)
            pltpu.make_async_remote_copy(
                src_ref=masked.at[to, part],
                dst_ref=quarters.at[y, part],
                send_sem=y_send,
                recv_sem=y_recv,
                device_id=(w, to),
                device_id_type=MESH,
            ).start()
    pltpu.make_async_copy(masked.at[y], quarters.at[y], y_recv).start()
    arrived(quarters, y_recv)
    for n in range(NY):
        out[n * FC : (n + 1) * FC] = quarters[n]

    arrived(masked.at[pl.ds(0, NY - 1)], y_send)
    arrived(source_in.at[pl.ds(0, PLANE - 1)], source_send)
    for group, (first, number) in enumerate(GROUPS):
        arrived(incoming.at[pl.ds(first, number), pl.ds(0, PLANE - 1)], send_sem.at[group])
    for m in range(HOPS - 1):
        arrived(half(*right[m]), right_send.at[m])
        arrived(half(*left[m]), left_send.at[m])
    for i in range(TAILS):
        arrived(tail(half(*right[last]), i), right_send.at[last + i])
        arrived(tail(half(*left[last]), i), left_send.at[last + i])

    @pl.loop(0, NZ)
    def _(plane):
        halo(plane).wait_send()


def masked_spectra(raw, filter_taps, dft, health, counts, source_index):
    bf16, f32 = jnp.bfloat16, jnp.float32
    dma = pltpu.SemaphoreType.DMA
    vmem = pl.BlockSpec(memory_space=pltpu.VMEM)
    whole = pl.BlockSpec(memory_space=pl.ANY)
    groups = len(GROUPS)
    return pl.pallas_call(
        spectra_kernel,
        out_shape=jax.ShapeDtypeStruct((F, SHARE, BLOCK_CH), bf16),
        in_specs=[whole, vmem, whole, whole, whole, whole],
        out_specs=vmem,
        scratch_shapes=[
            pltpu.VMEM((L, L), bf16),
            pltpu.VMEM((C // BLOCK_CH, BLOCK_CH), jnp.int32),
            pltpu.SMEM((C // BLOCK_CH,), jnp.int32),
            pltpu.SMEM((SRC,), jnp.int32),
            dma((4,)),
            pltpu.VMEM((STEPS, ROW, STEP_RAW), bf16),
            pltpu.VMEM((HALO, C), bf16),
            pltpu.VMEM((HALO, C // 2), bf16),
            pltpu.VMEM((HALO, C // 2), bf16),
            pltpu.VMEM((L, ROW), bf16),
            pltpu.VMEM((8, BLOCK_CH), f32),
            pltpu.VMEM((STEPS, L, STEP_CH), f32),
            pltpu.VMEM((F, BLOCK_CH), f32),
            pltpu.VMEM((1, BLOCK_CH), f32),
            pltpu.VMEM((2 * F, BLOCK_CH), f32),
            pltpu.VMEM((NZ, NXC, F, BLOCK_CH), bf16),
            pltpu.VMEM((NZ, PLANE, FC, BLOCK_CH), bf16),
            pltpu.VMEM((F, BLOCK_CH), bf16),
            pltpu.VMEM((PLANE, FC, BLOCK_CH), bf16),
            pltpu.VMEM((FC, PLANE, BLOCK_CH), bf16),
            pltpu.VMEM((FC, PLANE, BLOCK_CH), bf16),
            pltpu.VMEM((NZ, NY, FC, SHARE, BLOCK_CH), bf16),
            pltpu.VMEM((HOPS, 2, FC, SHARE, BLOCK_CH), bf16),
            pltpu.VMEM((HOPS, 2, FC, SHARE, BLOCK_CH), bf16),
            pltpu.VMEM((NY, FC, SHARE, BLOCK_CH), bf16),
            pltpu.VMEM((NY, FC, SHARE, BLOCK_CH), bf16),
            dma((STEPS,)),
            dma,
            dma((NZ,)),
            dma((NZ,)),
            dma((groups,)),
            dma((groups,)),
            dma,
            dma,
            dma((HOPS + TAILS - 1,)),
            dma((HOPS + TAILS - 1,)),
            dma((HOPS + TAILS - 1,)),
            dma((HOPS + TAILS - 1,)),
            dma,
            dma,
        ],
        compiler_params=pltpu.CompilerParams(
            collective_id=0, has_side_effects=True, vmem_limit_bytes=60 << 20
        ),
        name="masked_spectra",
    )(raw, filter_taps, dft, health, counts, source_index)


def lag_kernel(masked, table, out, by_source):
    step = pl.program_id(0)

    @pl.when(step == 0)
    def _():
        by_source[...] = jnp.swapaxes(masked[...], 0, 1)

    factor = 1.0 / math.sqrt(WIDE * NY * F)
    for k in range(out.shape[0]):
        turned = by_source[step * out.shape[0] + k].T
        out[k, :CAP] = factor * (
            jnp.dot(turned[:CAP], table[0], preferred_element_type=jnp.float32)
            + jnp.dot(turned[CAP:], table[1], preferred_element_type=jnp.float32)
        )
        out[k, CAP:] = jnp.zeros((BLOCK_CH - CAP, L), jnp.float32)


def correlations(masked, table):
    part = 4
    return pl.pallas_call(
        lag_kernel,
        grid=(SHARE // part,),
        out_shape=jax.ShapeDtypeStruct((SHARE, BLOCK_CH, L), jnp.float32),
        in_specs=[
            pl.BlockSpec((F, SHARE, BLOCK_CH), lambda i: (0, 0, 0)),
            pl.BlockSpec((2, F, L), lambda i: (0, 0, 0)),
        ],
        out_specs=pl.BlockSpec((part, BLOCK_CH, L), lambda i: (i, 0, 0)),
        scratch_shapes=[pltpu.VMEM((SHARE, F, BLOCK_CH), jnp.bfloat16)],
        compiler_params=pltpu.CompilerParams(vmem_limit_bytes=60 << 20),
        name="correlations",
    )(masked, table)


def body(raw_record, filter_taps, health_mask, counts, source_index):
    masked = masked_spectra(
        raw_record,
        filter_taps.reshape(1, K),
        jnp.asarray(dft_table()),
        health_mask.reshape(C // BLOCK_CH, BLOCK_CH),
        counts,
        source_index,
    )
    return correlations(masked, jnp.asarray(lag_table()))


def solution(mesh):
    placed = (P("narrow", "wide", None), P(), P(), P(), P())
    return jax.shard_map(
        body, mesh=mesh, in_specs=placed, out_specs=P("narrow", "wide", None), check_vma=False
    )
```

time: 98.1 us -> 82.5 us (0.84)
  Pallas kernels: 92.8 us -> 82.4 us
  local copies, waits for them, and re-layouts: 3.33 us -> 0 us
  other arithmetic: 1.72 us -> 0 us
    pallas_call x1, Pallas kernels: 90.2 us -> 78.7 us  [masked_spectra(): pl.pallas_call(spectra_kernel, out_shape=jax.ShapeDtypeStruct((F, SHARE,...]
    slice x2 -> x0, local copies, waits for them, and re-layouts: 1.42 us -> none  [the longest x1 0.76 us: body(): taps[:1:-1]]
    pallas_call x1, Pallas kernels: 2.57 us -> 3.64 us  [correlations(): pl.pallas_call(lag_kernel, grid=(SHARE // part,), out_shape=jax.ShapeDtyp...]
where the time goes in v2:
time: 82.5 us; the launch traced here: 82.4 us
  Pallas kernels  82.4 us (100%)
    pallas_call x1, Pallas kernels, masked_spectra(): pl.pallas_call(spectra_kernel, out_shape=jax.ShapeDtypeStruct((F, SHARE,...  78.7 us
    pallas_call x1, Pallas kernels, correlations(): pl.pallas_call(lag_kernel, grid=(SHARE // part,), out_shape=jax.ShapeDtyp...  3.64 us

profile of v2, /device:TPU:1, one launch (start us, length us, event | category | flops | bytes accessed | tf_op | source)
XLA Modules:
  0.0 82.4 jit_solution(1681639700108359649)
XLA Ops:
  0.0 78.7 %masked_spectra.1.masked = bf16[128,16,128]{2,1,0:T(8,128)(2,1)} custom-call(bf16[1,512,8192]{2,1,0:T(8,128)(2,1)} %raw.1, bf16[1,32]{1,0:T(2,128)(2,1)} %bitcast.3, bf16[256,256]{1,0:T(8,128)(2,1)} %constant.4.clone.dft_hbm, s32[64,128]{1,0:T(8,128)} %bitcast.2, s32[64]{0:T(128)} %counts_hbm.1, s32[64]{0:T(128)} %index_hbm.1), custom_call_target="tpu_custom_call" | custom-call | tf_op jit(solution)/shard_map/masked_spectra/pallas_call | solution.py:432
  78.8 3.6 %correlations.1 = f32[16,128,256]{2,1,0:T(8,128)} custom-call(bf16[128,16,128]{2,1,0:T(8,128)(2,1)} %masked_spectra.1.masked, bf16[2,128,256]{2,1,0:T(8,128)(2,1)} %constant.5.clone.table), custom_call_target="tpu_custom_call" | custom-call | tf_op jit(solution)/shard_map/correlations/pallas_call | solution.py:505

commit v3 on v2

--- a/solution.py
+++ b/solution.py
@@ -31,7 +31,7 @@
 ROW = L * Q
 MESH = pl.DeviceIdType.MESH
 Z_ORDER = (4, 3, 5, 2, 6, 1, 7, 0)
-GROUPS = ((0, 1), (1, 2), (3, 2), (5, 2), (7, 1))
+GROUPS = ((0, 1), (1, 2), (3, 2), (5, 3))
 HOPS = 7
 TAIL = 8
 TAILS = FC // TAIL
@@ -66,7 +66,7 @@
 
 def spectra_kernel(
     raw, filter_taps, dft_hbm, health_hbm, counts_hbm, index_hbm, out,
-    dft, health, counts, source_index, small_sem,
+    dft, health, counts, source_index, small_sem, slot_ids,
     samples, edge, edge_out, edge_in, taps, tap_row, decimated, level_acc, weight_acc, source_acc,
     outgoing, incoming, source_out, source_in, source_t, chan_t, sums, right_in, left_in,
     masked, quarters,
@@ -75,12 +75,12 @@
 ):
     w = lax.axis_index("wide")
     y = lax.axis_index("narrow")
-    z, xc = w // NXC, lax.rem(w, NXC)
+    z, xc = w >> 3, w & (NXC - 1)
     me = xc * NY + y
 
     def peer(t):
-        other = lax.rem(me + t, PLANE)
-        return other // NY, lax.rem(other, NY)
+        other = (me + t) & (PLANE - 1)
+        return other >> 2, other & (NY - 1)
 
     edge_copy = pltpu.make_async_copy(raw.at[0, pl.ds(ROW - HALO, HALO)], edge, edge_sem)
     edge_copy.start()
@@ -168,13 +168,15 @@
     halo_taps = halo_taps.astype(jnp.bfloat16)
 
     lane = lanes((1, BLOCK_CH))
-    slot_lane = lax.rem(lane, CAP)
+    slot_lane = lane & (CAP - 1)
     for copy in small:
         copy.wait()
     source_row = jnp.zeros((1, BLOCK_CH), jnp.int32)
     for k in range(SRC):
         source_row = jnp.where(slot_lane == k, source_index[k], source_row)
 
+    slots = lax.broadcasted_iota(jnp.int32, (STEP_CH, BLOCK_CH), 0)
+    slot_ids[...] = 2 * slots - (slots & (CAP - 1))
     level_acc[...] = jnp.zeros_like(level_acc)
     weight_acc[...] = jnp.zeros_like(weight_acc)
     source_acc[...] = jnp.zeros_like(source_acc)
@@ -218,9 +220,8 @@
                 jnp.bfloat16
             )
         level_acc[...] = total
-        slots = lax.broadcasted_iota(jnp.int32, (STEP_CH, BLOCK_CH), 0)
-        ids = (2 * first + slots // CAP) * BLOCK_CH + lax.rem(slots, CAP)
-        chosen = (ids == source_row).astype(jnp.float32).astype(jnp.bfloat16)
+        chosen = jnp.where(slot_ids[...] == source_row - plane * STEP_RAW, 1.0, 0.0)
+        chosen = chosen.astype(jnp.bfloat16)
         source_acc[...] += jnp.dot(
             spectra.astype(jnp.bfloat16), chosen, preferred_element_type=jnp.float32
         )
@@ -284,15 +285,19 @@
                     held[q * GROUP : (q + 1) * GROUP, f * GROUP : (f + 1) * GROUP, :], 0, 1
                 )
 
+    arrived(incoming.at[pl.ds(*GROUPS[0])], recv_sem.at[0])
+    by_bin(incoming.at[0], chan_t)
     arrived(source_in, source_recv)
     by_bin(source_in, source_t)
     sign = jnp.where(lanes((SRC, BLOCK_CH)) < CAP, 1.0, -1.0)
 
     def cross_slots(group):
         first, number = GROUPS[group]
-        arrived(incoming.at[pl.ds(first, number)], recv_sem.at[group])
+        if first > 0:
+            arrived(incoming.at[pl.ds(first, number)], recv_sem.at[group])
         for slot in range(first, first + number):
-            by_bin(incoming.at[slot], chan_t)
+            if slot > 0:
+                by_bin(incoming.at[slot], chan_t)
 
             @pl.loop(0, FC // 8)
             def _(g, slot=slot):
@@ -356,14 +361,12 @@
     forward(1)
     forward(2)
     send_group(3)
-    send_group(4)
     cross_slots(2)
     forward(3)
     forward(4)
     cross_slots(3)
     forward(5)
     forward(6)
-    cross_slots(4)
 
     alive = jnp.where(slot_lane < counts[w], health[pl.ds(w, 1), :], 0)
     alive = jnp.where(lane < CAP, alive, pltpu.roll(alive, CAP, 1)).astype(jnp.float32)
@@ -440,6 +443,7 @@
             pltpu.SMEM((C // BLOCK_CH,), jnp.int32),
             pltpu.SMEM((SRC,), jnp.int32),
             dma((4,)),
+            pltpu.VMEM((STEP_CH, BLOCK_CH), jnp.int32),
             pltpu.VMEM((STEPS, ROW, STEP_RAW), bf16),
             pltpu.VMEM((HALO, C), bf16),
             pltpu.VMEM((HALO, C // 2), bf16),
@@ -501,7 +505,7 @@
 
 
 def correlations(masked, table):
-    part = 4
+    part = 8
     return pl.pallas_call(
         lag_kernel,
         grid=(SHARE // part,),

time: 82.5 us -> 81.3 us (0.985)
  Pallas kernels: 82.4 us -> 81.2 us
where the time goes in v3:
time: 81.3 us; the launch traced here: 81.2 us
  Pallas kernels  81.2 us (100%)
    pallas_call x1, Pallas kernels, masked_spectra(): pl.pallas_call(spectra_kernel, out_shape=jax.ShapeDtypeStruct((F, SHARE,...  78.3 us
    pallas_call x1, Pallas kernels, correlations(): pl.pallas_call(lag_kernel, grid=(SHARE // part,), out_shape=jax.ShapeDtyp...  2.9 us

profile of v3, /device:TPU:1, one launch (start us, length us, event | category | flops | bytes accessed | tf_op | source)
XLA Modules:
  0.0 81.2 jit_solution(17241608949717891009)
XLA Ops:
  0.0 78.3 %masked_spectra.1.masked = bf16[128,16,128]{2,1,0:T(8,128)(2,1)} custom-call(bf16[1,512,8192]{2,1,0:T(8,128)(2,1)} %raw.1, bf16[1,32]{1,0:T(2,128)(2,1)} %bitcast.3, bf16[256,256]{1,0:T(8,128)(2,1)} %constant.4.clone.dft_hbm, s32[64,128]{1,0:T(8,128)} %bitcast.2, s32[64]{0:T(128)} %counts_hbm.1, s32[64]{0:T(128)} %index_hbm.1), custom_call_target="tpu_custom_call" | custom-call | tf_op jit(solution)/shard_map/masked_spectra/pallas_call | solution.py:435
  78.3 2.9 %correlations.1 = f32[16,128,256]{2,1,0:T(8,128)} custom-call(bf16[128,16,128]{2,1,0:T(8,128)(2,1)} %masked_spectra.1.masked, bf16[2,128,256]{2,1,0:T(8,128)(2,1)} %constant.5.clone.table), custom_call_target="tpu_custom_call" | custom-call | tf_op jit(solution)/shard_map/correlations/pallas_call | solution.py:509

commit v4 on v3

--- a/solution.py
+++ b/solution.py
@@ -407,8 +407,12 @@
             ).start()
     pltpu.make_async_copy(masked.at[y], quarters.at[y], y_recv).start()
     arrived(quarters, y_recv)
-    for n in range(NY):
-        out[n * FC : (n + 1) * FC] = quarters[n]
+    results = [
+        pltpu.make_async_copy(quarters.at[n], out.at[pl.ds(n * FC, FC)], small_sem.at[n])
+        for n in range(NY)
+    ]
+    for copy in results:
+        copy.start()
 
     arrived(masked.at[pl.ds(0, NY - 1)], y_send)
     arrived(source_in.at[pl.ds(0, PLANE - 1)], source_send)
@@ -425,6 +429,9 @@
     def _(plane):
         halo(plane).wait_send()
 
+    for copy in results:
+        copy.wait()
+
 
 def masked_spectra(raw, filter_taps, dft, health, counts, source_index):
     bf16, f32 = jnp.bfloat16, jnp.float32
@@ -436,7 +443,7 @@
         spectra_kernel,
         out_shape=jax.ShapeDtypeStruct((F, SHARE, BLOCK_CH), bf16),
         in_specs=[whole, vmem, whole, whole, whole, whole],
-        out_specs=vmem,
+        out_specs=whole,
         scratch_shapes=[
             pltpu.VMEM((L, L), bf16),
             pltpu.VMEM((C // BLOCK_CH, BLOCK_CH), jnp.int32),

time: 81.3 us -> 81.3 us (level)
  no operation moved by 1% of the time
where the time goes in v4:
time: 81.3 us; the launch traced here: 81.2 us
  Pallas kernels  81.2 us (100%)
    pallas_call x1, Pallas kernels, masked_spectra(): pl.pallas_call(spectra_kernel, out_shape=jax.ShapeDtypeStruct((F, SHARE,...  78.3 us
    pallas_call x1, Pallas kernels, correlations(): pl.pallas_call(lag_kernel, grid=(SHARE // part,), out_shape=jax.ShapeDtyp...  2.9 us

profile of v4, /device:TPU:1, one launch (start us, length us, event | category | flops | bytes accessed | tf_op | source)
XLA Modules:
  0.0 81.2 jit_solution(3611377150286536007)
XLA Ops:
  0.0 78.3 %masked_spectra.1.masked = bf16[128,16,128]{2,1,0:T(8,128)(2,1)} custom-call(bf16[1,512,8192]{2,1,0:T(8,128)(2,1)} %raw.1, bf16[1,32]{1,0:T(2,128)(2,1)} %bitcast.3, bf16[256,256]{1,0:T(8,128)(2,1)} %constant.4.clone.dft_hbm, s32[64,128]{1,0:T(8,128)} %bitcast.2, s32[64]{0:T(128)} %counts_hbm.1, s32[64]{0:T(128)} %index_hbm.1), custom_call_target="tpu_custom_call" | custom-call | tf_op jit(solution)/shard_map/masked_spectra/pallas_call | solution.py:442
  78.3 2.9 %correlations.1 = f32[16,128,256]{2,1,0:T(8,128)} custom-call(bf16[128,16,128]{2,1,0:T(8,128)(2,1)} %masked_spectra.1.masked, bf16[2,128,256]{2,1,0:T(8,128)(2,1)} %constant.5.clone.table), custom_call_target="tpu_custom_call" | custom-call | tf_op jit(solution)/shard_map/correlations/pallas_call | solution.py:516
